TPU v7x, 32 devices: a whole 2x2x4 slice. The times are simulated.
32 devices in a mesh: row: 4 (over z), col: 8 (over y, x, core).
Axes of the slice: x: 2, y: 2, z: 4, core: 2. Of those that a mesh axis runs over, the one named last changes fastest.
Arguments:
- pair_counts: float32 [32, 32, 2, 128, 128], P(('row', 'col')), may hold values from 0.01 to 30
- tile_index: int32 [32, 32, 2], P(('row', 'col')), may hold values from 0 to 255
- slot_counts: int32 [32, 32], P(('row', 'col')), may hold values from 0 to 2, as said below
- row_totals: int32 [8192], P('row'), may hold values from 1000 to 59999
- col_totals: int32 [16384], P('col'), may hold values from 1000 to 59999
- sketch: bfloat16 [16384, 128], P('col'), may hold values from -0.046875 to 0.046875
Outputs:
- range_rows: bfloat16 [8192, 128], P('row')
- corange: bfloat16 [16384, 128], P('col')
Inputs may be any that keep to these rules, and one draw needn't show every extreme that they name: `slot_counts`: slot counts from a shard to an owner; for some owners every shard fills all 2 slots. `tile_index`: tile positions may repeat; repeated tiles add.
All inputs are finite; a program needn't handle non-finite values.
Results may differ from a plain program's by a relative error of at most 0.001.
The roundings to bfloat16 on the way count: a program that leaves them out, or rounds other values in their place, can miss the bound.
Values may be sent and summed in bfloat16 or wider, within the bound.
A program may use at most 128 MiB of HBM per device.

v0:
```python
import math
import jax
import jax.numpy as jnp
from jax import lax
from jax.sharding import PartitionSpec as P

TILE = 128
RT_DEV = 16
CT_DEV = 16
log_shift = 0.25


def pmi_block(tiles, parked, row_here, col_here, grand):
    ntiles = RT_DEV * CT_DEV
    stack = jnp.zeros((ntiles + 1, TILE, TILE), jnp.float32).at[parked].add(tiles)[:ntiles]
    counts_block = (
        stack.reshape(RT_DEV, CT_DEV, TILE, TILE)
        .transpose(0, 2, 1, 3)
        .reshape(RT_DEV * TILE, CT_DEV * TILE)
    )
    scaled = (
        counts_block
        * grand
        / (row_here.astype(jnp.float32)[:, None] * col_here.astype(jnp.float32)[None, :])
    )
    return jnp.maximum(jnp.log1p(scaled) - log_shift, 0.0).astype(jnp.bfloat16)


def on_device(pair_counts, tile_index, slot_counts, row_totals, col_totals, sketch):
    row_count = lax.axis_size("row")
    slots = lax.broadcasted_iota(jnp.int32, tile_index.shape, 2)
    parked = jnp.where(slots < slot_counts[:, :, None], tile_index, RT_DEV * CT_DEV)
    grand = lax.psum(jnp.sum(row_totals.astype(jnp.float32)), "row")
    arrived, places = (
        lax.all_to_all(pair_counts, ("row", "col"), split_axis=1, concat_axis=0, tiled=True),
        lax.all_to_all(parked, ("row", "col"), split_axis=1, concat_axis=0, tiled=True),
    )
    pmi = pmi_block(
        arrived.reshape(-1, TILE, TILE), places.reshape(-1), row_totals, col_totals, grand
    )
    partial_rows = jnp.dot(pmi, sketch, preferred_element_type=jnp.float32)
    range_rows = lax.psum(partial_rows, "col").astype(jnp.bfloat16)
    partial_cols = lax.dot_general(
        pmi, range_rows, (((0,), (0,)), ((), ())), preferred_element_type=jnp.float32
    )
    col_sums = lax.psum(partial_cols, "row")
    total_rows = pmi.shape[0] * row_count
    corange = (col_sums / math.sqrt(total_rows)).astype(jnp.bfloat16)
    return (range_rows, corange)


def solution(mesh):
    placed = (
        P(("row", "col"), None, None, None, None),
        P(("row", "col"), None, None),
        P(("row", "col"), None),
        P("row"),
        P("col"),
        P("col", None),
    )
    return jax.shard_map(
        on_device,
        mesh=mesh,
        in_specs=placed,
        out_specs=(P("row", None), P("col", None)),
        check_vma=False,
    )
```

profile of v0, /device:TPU:0, one launch (start us, length us, event | category | flops | bytes accessed | tf_op | source)
XLA Modules:
  0.0 312.3 jit_solution(12001681732545011220)
XLA Ops:
  7.2 0.0 copy-start
  7.2 0.7 compare_select_fusion.1
  7.9 0.1 copy.17
  8.0 14.2 %all_to_all.8 = s32[1,32,2]{2,0,1:T(1,128)S(1)} all-to-all(s32[1,32,2]{2,0,1:T(1,128)S(1)} %copy.17), channel_id=1, replica_groups=mesh['row'=4,'col'=8] {'row','col'}, dimensions={1} | all-to-all | bytes 512 | tf_op jit(solution)/shard_map/all_to_all | solution.py:36
  22.3 3.6 %all-to-all-start.1 = ((f32[1,32,2,128,128]{4,3,2,0,1:T(8,128)}), f32[1,32,2,128,128]{4,3,2,0,1:T(8,128)}, u32[]{:S(2)}, u32[]{:S(2)}) async-start(f32[1,32,2,128,128]{4,3,2,0,1:T(8,128)} %bitcast.27), calls=%async_computation.1 | async-start | bytes 8388608 | tf_op jit(solution)/shard_map/all_to_all | solution.py:35
  25.8 0.0 all-reduce.3.cloned.1.call-start
  25.9 1.3 convert_reduce_fusion
  27.2 74.1 %psum.21 = f32[]{:T(128)} all-reduce(f32[]{:T(128)} %convert_reduce_fusion), channel_id=1, replica_groups=mesh['row'=4,'col'=8] {'row'}, use_global_device_ids=true, to_apply=%region_2.3 | all-reduce | flops 1 | bytes 8 | tf_op jit(solution)/shard_map/psum | solution.py:33
  101.3 0.7 convert_element_type.16
  102.0 0.7 convert_element_type.17
  102.7 0.5 broadcast.52
  103.2 0.7 reduce.3
  103.9 0.1 reshape.89
  104.0 16.0 %all-to-all-done.1 = f32[1,32,2,128,128]{4,3,2,0,1:T(8,128)} async-done(((f32[1,32,2,128,128]{4,3,2,0,1:T(8,128)}), f32[1,32,2,128,128]{4,3,2,0,1:T(8,128)}, u32[]{:S(2)}, u32[]{:S(2)}) %all-to-all-start.1) | async-done | bytes 4194336 | tf_op jit(solution)/shard_map/all_to_all | solution.py:35
  120.1 7.9 %broadcast_in_dim.6 = f32[257,128,128]{2,1,0:T(8,128)} broadcast(f32[]{:T(128)} %constant.6.clone.1), dimensions={} | broadcast | bytes 16842756 | tf_op jit(solution)/shard_map/broadcast_in_dim | solution.py:15
  128.0 13.3 %scatter_fusion = f32[257,128,128]{2,1,0:T(8,128)} fusion(f32[257,128,128]{2,1,0:T(8,128)} %broadcast_in_dim.6, s32[64]{0:T(128)S(1)} %fusion.4, f32[64,128,128]{2,1,0:T(8,128)} %bitcast.3), kind=kCustom, calls=%fused_computation | custom fusion | flops 1048576 | bytes 12583168 | tf_op jit(solution)/shard_map/scatter-add | solution.py:15
  141.3 7.2 %slice_multiply_fusion = f32[256,128,128]{2,1,0:T(8,128)S(1)} fusion(f32[257,128,128]{2,1,0:T(8,128)} %scatter_fusion, f32[]{:T(128)} %psum.21), kind=kLoop, calls=%fused_computation.5 | loop fusion | flops 4194304 | bytes 33554436 | tf_op jit(solution)/shard_map/mul | solution.py:22
  148.5 21.4 %copy.19 = f32[16,128,16,128]{3,2,1,0:T(8,128)S(1)} copy(f32[16,128,16,128]{3,1,2,0:T(8,128)S(1)} %bitcast.26) | data formatting | bytes 33554432 | tf_op jit(solution)/shard_map/mul | solution.py:22
  169.9 13.8 %fusion.3 = bf16[2048,2048]{1,0:T(8,128)(2,1)S(1)} fusion(f32[256,8,16,128]{3,2,1,0:T(8,128)S(1)} %bitcast.25, f32[2048]{0:T(1024)S(1)} %convert_element_type.17, f32[2048]{0:T(1024)S(1)} %convert_element_type.16), kind=kLoop, calls=%fused_computation.6 | loop fusion | flops 20971520 | bytes 25182208 | tf_op jit(solution)/shard_map/convert_element_type | solution.py:26
  183.7 0.0 copy-start.1
  183.7 3.2 %copy-done.1 = bf16[2048,2048]{1,0:T(8,128)(2,1)} copy-done((bf16[2048,2048]{1,0:T(8,128)(2,1)}, bf16[2048,2048]{1,0:T(8,128)(2,1)S(1)}, u32[]{:S(2)}) %copy-start.1) | copy-done | bytes 8388632
  187.0 0.0 copy-done
  187.0 2.3 fusion.5
  189.3 51.8 %all-reduce.4 = bf16[2048,128]{1,0:T(8,128)(2,1)S(1)} all-reduce(f32[2048,128]{1,0:T(8,128)S(1)} %fusion.5), channel_id=1, replica_groups=mesh['row'=4,'col'=8] {'col'}, use_global_device_ids=true, to_apply=%region_3.4 | all-reduce | flops 262144 | bytes 1572864 | tf_op jit(solution)/shard_map/psum | solution.py:42
  241.1 0.0 copy-start.2
  241.1 7.0 %fusion.6 = f32[2048,128]{1,0:T(8,128)} fusion(bf16[2048,2048]{1,0:T(8,128)(2,1)} %copy-done.1, bf16[2048,128]{1,0:T(8,128)(2,1)S(1)} %all-reduce.4), kind=kOutput, calls=%fused_computation.13 | convolution fusion | flops 1073741824 | bytes 9961472 | tf_op jit(solution)/shard_map/dot_general | solution.py:43
  248.1 0.0 all-reduce.3.cloned.1.call-update
  248.2 55.2 %all-reduce.3.cloned.1.call-done = f32[2048,128]{1,0:T(8,128)} async-done(((f32[2048,128]{1,0:T(8,128)}), f32[2048,128]{1,0:T(8,128)}) %all-reduce.3.cloned.1.call-update) | async-done | bytes 1048592 | tf_op jit(solution)/shard_map/psum | solution.py:46
  303.4 2.1 multiply_convert_fusion
  305.5 0.0 copy-done.2
  (1 shorter events, 0.0 us)
Async XLA Ops:
  7.2 179.8 %copy-start = (bf16[2048,128]{1,0:T(8,128)(2,1)S(1)}, bf16[2048,128]{1,0:T(8,128)(2,1)}, u32[]{:S(2)}) copy-start(bf16[2048,128]{1,0:T(8,128)(2,1)} %param.11) | copy-start | bytes 1572868
  22.3 97.8 %all-to-all-start.1 = ((f32[1,32,2,128,128]{4,3,2,0,1:T(8,128)}), f32[1,32,2,128,128]{4,3,2,0,1:T(8,128)}, u32[]{:S(2)}, u32[]{:S(2)}) async-start(f32[1,32,2,128,128]{4,3,2,0,1:T(8,128)} %bitcast.27), calls=%async_computation.1 | async-start | bytes 8388608 | tf_op jit(solution)/shard_map/all_to_all | solution.py:35
  25.8 277.5 %all-reduce.3.cloned.1.call-start = ((), (), s32[]{:S(2)}) async-start(), calls=%async_computation.2 | async-start | bytes 2097152 | tf_op jit(solution)/shard_map/psum | solution.py:46
  183.7 3.2 %copy-start.1 = (bf16[2048,2048]{1,0:T(8,128)(2,1)}, bf16[2048,2048]{1,0:T(8,128)(2,1)S(1)}, u32[]{:S(2)}) copy-start(bf16[2048,2048]{1,0:T(8,128)(2,1)S(1)} %fusion.3) | copy-start | bytes 25165828
  241.1 64.4 %copy-start.2 = (bf16[2048,128]{1,0:T(8,128)(2,1)}, bf16[2048,128]{1,0:T(8,128)(2,1)S(1)}, u32[]{:S(2)}) copy-start(bf16[2048,128]{1,0:T(8,128)(2,1)S(1)} %all-reduce.4) | copy-start | bytes 1572868
Sparse Core Ops, SparseCore 0:
  248.3 55.0 all-reduce.2
where the time goes:
time: 313 us; the launch traced here: 312 us
  blocking collectives  140 us (45%)
  waiting for transfers between devices  71.2 us (23%)
  other arithmetic  40.6 us (13%)
  local copies, waits for them, and re-layouts  33.2 us (11%)
  between operations  14.1 us (5%)
  matrix products  9.36 us (3%)
  starting transfers between devices  3.63 us (1%)
    psum x1, blocking collectives, on_device(): grand = lax.psum(jnp.sum(row_totals.astype(jnp.float32)), 'row')  74.1 us
    psum x1, waiting for transfers between devices, on_device(): col_sums = lax.psum(partial_cols, 'row')  55.2 us
    psum x1, blocking collectives, on_device(): range_rows = lax.psum(partial_rows, 'col').astype(jnp.bfloat16)  51.8 us
    mul x1, local copies, waits for them, and re-layouts, pmi_block(): counts_block * grand  21.4 us
    all_to_all x1, waiting for transfers between devices, on_device(): lax.all_to_all(pair_counts, ('row', 'col'), split_axis=1, concat_axis=0,...  16 us
    all_to_all x1, blocking collectives, on_device(): lax.all_to_all(parked, ('row', 'col'), split_axis=1, concat_axis=0, tiled...  14.2 us
    convert_element_type x1, other arithmetic, pmi_block(): return jnp.maximum(jnp.log1p(scaled) - log_shift, 0.0).astype(jnp.bfloat16)  13.8 us
    scatter-add x1, other arithmetic, pmi_block(): jnp.zeros((ntiles + 1, TILE, TILE), jnp.float32).at[parked].add(tiles)  13.3 us
  transfers between devices with their start and end apart: 2, of which 2 were waited for; matrix products, arithmetic and copies ran while one was open for 1% of the time, Pallas kernels for 0%

commit v1 on v0

--- a/solution.py
+++ b/solution.py
@@ -32,7 +32,15 @@
     parked = jnp.where(slots < slot_counts[:, :, None], tile_index, RT_DEV * CT_DEV)
     grand = lax.psum(jnp.sum(row_totals.astype(jnp.float32)), "row")
     arrived, places = (
-        lax.all_to_all(pair_counts, ("row", "col"), split_axis=1, concat_axis=0, tiled=True),
+        jnp.concatenate(
+            lax.all_to_all(
+                jnp.stack(jnp.split(pair_counts, lax.axis_size(("row", "col")), axis=1)),
+                ("row", "col"),
+                0,
+                0,
+            ),
+            axis=0,
+        ),
         lax.all_to_all(parked, ("row", "col"), split_axis=1, concat_axis=0, tiled=True),
     )
     pmi = pmi_block(

time: 313 us -> 358 us (1.14)
  local copies, waits for them, and re-layouts: 33.2 us -> 83.8 us
  blocking collectives: 140 us -> 127 us
  starting transfers between devices: 3.63 us -> 13.3 us
    unnamed x6 -> x41, local copies, waits for them, and re-layouts: 3.23 us -> 51.6 us
    all_to_all x1 -> x0, blocking collectives: 14.2 us -> none  [on_device(): lax.all_to_all(parked, ('row', 'col'), split_axis=1, concat_axis=0, tiled...]
    all_to_all x1 -> x2, starting transfers between devices: 3.58 us -> 13.3 us  [the longest x1 7.3 us: on_device(): lax.all_to_all(parked, ('row', 'col'), split_axis=1, concat_axis=0, tiled...]
    all_to_all x1 -> x2, waiting for transfers between devices: 16 us -> 16.9 us  [the longest x1 16.9 us: on_device(): lax.all_to_all(jnp.stack(jnp.split(pair_counts, lax.axis_size(('row', 'co...]
  transfers between devices with their start and end apart: 2 -> 3, of which waited for: 2 -> 2; matrix products, arithmetic and copies ran while one was open for 1% -> 15% of each run, Pallas kernels for 0% -> 0%
where the time goes in v1:
time: 358 us; the launch traced here: 357 us
  blocking collectives  127 us (35%)
  local copies, waits for them, and re-layouts  83.8 us (23%)
  waiting for transfers between devices  70.8 us (20%)
  other arithmetic  38.5 us (11%)
  between operations  14.2 us (4%)
  starting transfers between devices  13.3 us (4%)
  matrix products  9.36 us (3%)
    psum x1, blocking collectives, on_device(): grand = lax.psum(jnp.sum(row_totals.astype(jnp.float32)), 'row')  75.2 us
    psum x1, waiting for transfers between devices, on_device(): col_sums = lax.psum(partial_cols, 'row')  53.9 us
    psum x1, blocking collectives, on_device(): range_rows = lax.psum(partial_rows, 'col').astype(jnp.bfloat16)  51.9 us
    unnamed x41, local copies, waits for them, and re-layouts  51.6 us
    mul x1, local copies, waits for them, and re-layouts, pmi_block(): counts_block * grand  21.4 us
    all_to_all x1, waiting for transfers between devices, on_device(): lax.all_to_all(jnp.stack(jnp.split(pair_counts, lax.axis_size(('row', 'co...  16.9 us
    convert_element_type x1, other arithmetic, pmi_block(): return jnp.maximum(jnp.log1p(scaled) - log_shift, 0.0).astype(jnp.bfloat16)  13.8 us
    scatter-add x1, other arithmetic, pmi_block(): jnp.zeros((ntiles + 1, TILE, TILE), jnp.float32).at[parked].add(tiles)  13.3 us
  transfers between devices with their start and end apart: 3, of which 2 were waited for; matrix products, arithmetic and copies ran while one was open for 15% of the time, Pallas kernels for 0%

profile of v1, /device:TPU:0, one launch (start us, length us, event | category | flops | bytes accessed | tf_op | source)
XLA Modules:
  0.0 356.9 jit_solution(6709724823019802386)
XLA Ops:
  8.6 7.3 %all-to-all-start = ((s32[1,32,2]{2,0,1:T(1,128)}), s32[1,32,2]{2,0,1:T(1,128)S(1)}, u32[]{:S(2)}, u32[]{:S(2)}) async-start(s32[1,32,2]{2,0,1:T(1,128)} %copy.16), calls=%async_computation | async-start | bytes 32768 | tf_op jit(solution)/shard_map/all_to_all | solution.py:44
  17.5 1.6 bitcast_dynamic-update-slice_fusion.30
  19.0 1.6 bitcast_dynamic-update-slice_fusion.29
  20.6 1.6 bitcast_dynamic-update-slice_fusion.28
  22.2 1.6 bitcast_dynamic-update-slice_fusion.27
  25.3 1.6 bitcast_dynamic-update-slice_fusion.25
  26.9 1.6 bitcast_dynamic-update-slice_fusion.24
  30.0 1.6 bitcast_dynamic-update-slice_fusion.22
  33.1 1.6 bitcast_dynamic-update-slice_fusion.20
  36.2 1.6 bitcast_dynamic-update-slice_fusion.18
  39.3 1.6 bitcast_dynamic-update-slice_fusion.16
  40.9 1.6 bitcast_dynamic-update-slice_fusion.15
  45.6 1.6 bitcast_dynamic-update-slice_fusion.12
  48.7 1.6 bitcast_dynamic-update-slice_fusion.10
  51.8 1.6 bitcast_dynamic-update-slice_fusion.8
  55.0 1.6 bitcast_dynamic-update-slice_fusion.6
  56.5 1.6 bitcast_dynamic-update-slice_fusion.5
  64.3 1.6 bitcast_dynamic-update-slice_fusion
  65.9 6.0 %all-to-all-start.1 = ((f32[32,1,1,2,128,128]{5,4,3,2,1,0:T(8,128)}), f32[32,1,1,2,128,128]{5,4,3,2,1,0:T(8,128)}, u32[]{:S(2)}, u32[]{:S(2)}) async-start(f32[32,1,1,2,128,128]{5,4,3,2,1,0:T(8,128)} %bitcast_dynamic-update-slice_fusion), calls=%async_computation.1 | async-start | bytes 8388608 | tf_op jit(solution)/shard_map/all_to_all | solution.py:36
  72.5 75.2 %psum.21 = f32[]{:T(128)} all-reduce(f32[]{:T(128)} %convert_reduce_fusion), channel_id=1, replica_groups=mesh['row'=4,'col'=8] {'row'}, use_global_device_ids=true, to_apply=%region_2.3 | all-reduce | flops 1 | bytes 8 | tf_op jit(solution)/shard_map/psum | solution.py:33
  149.0 16.9 %all-to-all-done.1 = f32[32,1,1,2,128,128]{5,4,3,2,1,0:T(8,128)} async-done(((f32[32,1,1,2,128,128]{5,4,3,2,1,0:T(8,128)}), f32[32,1,1,2,128,128]{5,4,3,2,1,0:T(8,128)}, u32[]{:S(2)}, u32[]{:S(2)}) %all-to-all-start.1) | async-done | bytes 4194336 | tf_op jit(solution)/shard_map/all_to_all | solution.py:36
  165.9 7.9 %broadcast_in_dim.6 = f32[257,128,128]{2,1,0:T(8,128)} broadcast(f32[]{:T(128)} %constant.6.clone.1), dimensions={} | broadcast | bytes 16842756 | tf_op jit(solution)/shard_map/broadcast_in_dim | solution.py:15
  173.8 13.3 %scatter_fusion = f32[257,128,128]{2,1,0:T(8,128)} fusion(f32[257,128,128]{2,1,0:T(8,128)} %broadcast_in_dim.6, s32[64]{0:T(128)S(1)} %fusion.4, f32[64,128,128]{2,1,0:T(8,128)} %bitcast.34), kind=kCustom, calls=%fused_computation | custom fusion | flops 1048576 | bytes 12583168 | tf_op jit(solution)/shard_map/scatter-add | solution.py:15
  187.1 7.2 %slice_multiply_fusion = f32[256,128,128]{2,1,0:T(8,128)S(1)} fusion(f32[257,128,128]{2,1,0:T(8,128)} %scatter_fusion, f32[]{:T(128)} %psum.21), kind=kLoop, calls=%fused_computation.5 | loop fusion | flops 4194304 | bytes 33554436 | tf_op jit(solution)/shard_map/mul | solution.py:22
  194.3 21.4 %copy.17 = f32[16,128,16,128]{3,2,1,0:T(8,128)S(1)} copy(f32[16,128,16,128]{3,1,2,0:T(8,128)S(1)} %bitcast.89) | data formatting | bytes 33554432 | tf_op jit(solution)/shard_map/mul | solution.py:22
  215.7 13.8 %fusion.3 = bf16[2048,2048]{1,0:T(8,128)(2,1)S(1)} fusion(f32[256,8,16,128]{3,2,1,0:T(8,128)S(1)} %bitcast.88, f32[2048]{0:T(1024)S(1)} %convert_element_type.17, f32[2048]{0:T(1024)S(1)} %convert_element_type.16), kind=kLoop, calls=%fused_computation.6 | loop fusion | flops 20971520 | bytes 25182208 | tf_op jit(solution)/shard_map/convert_element_type | solution.py:26
  229.6 3.2 copy-done.1
  232.8 2.3 fusion.5
  235.2 51.9 %all-reduce.4 = bf16[2048,128]{1,0:T(8,128)(2,1)S(1)} all-reduce(f32[2048,128]{1,0:T(8,128)S(1)} %fusion.5), channel_id=1, replica_groups=mesh['row'=4,'col'=8] {'col'}, use_global_device_ids=true, to_apply=%region_3.4 | all-reduce | flops 262144 | bytes 1572864 | tf_op jit(solution)/shard_map/psum | solution.py:50
  287.1 7.0 %fusion.6 = f32[2048,128]{1,0:T(8,128)} fusion(bf16[2048,2048]{1,0:T(8,128)(2,1)} %copy-done.1, bf16[2048,128]{1,0:T(8,128)(2,1)S(1)} %all-reduce.4), kind=kOutput, calls=%fused_computation.45 | convolution fusion | flops 1073741824 | bytes 9961472 | tf_op jit(solution)/shard_map/dot_general | solution.py:51
  294.1 53.9 %all-reduce.3.cloned.1.call-done = f32[2048,128]{1,0:T(8,128)} async-done(((f32[2048,128]{1,0:T(8,128)}), f32[2048,128]{1,0:T(8,128)}) %all-reduce.3.cloned.1.call-update) | async-done | bytes 1048592 | tf_op jit(solution)/shard_map/psum | solution.py:54
  348.0 2.1 multiply_convert_fusion
  (36 shorter events, 26.7 us)
Async XLA Ops:
  7.2 225.7 %copy-start = (bf16[2048,128]{1,0:T(8,128)(2,1)S(1)}, bf16[2048,128]{1,0:T(8,128)(2,1)}, u32[]{:S(2)}) copy-start(bf16[2048,128]{1,0:T(8,128)(2,1)} %param.11) | copy-start | bytes 1572868
  8.6 57.3 %all-to-all-start = ((s32[1,32,2]{2,0,1:T(1,128)}), s32[1,32,2]{2,0,1:T(1,128)S(1)}, u32[]{:S(2)}, u32[]{:S(2)}) async-start(s32[1,32,2]{2,0,1:T(1,128)} %copy.16), calls=%async_computation | async-start | bytes 32768 | tf_op jit(solution)/shard_map/all_to_all | solution.py:44
  65.9 6.0 %copy-start.3 = (s32[2048]{0:T(1024)S(1)}, s32[2048]{0:T(1024)}, u32[]{:S(2)}) copy-start(s32[2048]{0:T(1024)} %param.9) | copy-start | bytes 24580
  65.9 81.8 %copy-start.4 = (s32[2048]{0:T(1024)S(1)}, s32[2048]{0:T(1024)}, u32[]{:S(2)}) copy-start(s32[2048]{0:T(1024)} %param.10) | copy-start | bytes 24580
  65.9 100.1 %all-to-all-start.1 = ((f32[32,1,1,2,128,128]{5,4,3,2,1,0:T(8,128)}), f32[32,1,1,2,128,128]{5,4,3,2,1,0:T(8,128)}, u32[]{:S(2)}, u32[]{:S(2)}) async-start(f32[32,1,1,2,128,128]{5,4,3,2,1,0:T(8,128)} %bitcast_dynamic-update-slice_fusion), calls=%async_computation.1 | async-start | bytes 8388608 | tf_op jit(solution)/shard_map/all_to_all | solution.py:36
  71.8 276.1 %all-reduce.3.cloned.1.call-start = ((), (), s32[]{:S(2)}) async-start(), calls=%async_computation.2 | async-start | bytes 2097152 | tf_op jit(solution)/shard_map/psum | solution.py:54
  229.6 3.2 copy-start.1
  287.1 7.0 %copy-start.2 = (bf16[2048,128]{1,0:T(8,128)(2,1)}, bf16[2048,128]{1,0:T(8,128)(2,1)S(1)}, u32[]{:S(2)}) copy-start(bf16[2048,128]{1,0:T(8,128)(2,1)S(1)} %all-reduce.4) | copy-start | bytes 1572868
Sparse Core Ops, SparseCore 0:
  294.2 53.6 all-reduce.2
